TPU v7x, 256 devices: a whole 4x4x8 slice. The times are simulated.
256 devices in a mesh: row: 16 (over y, z_lo, core), col: 16 (over z_hi, x).
Axes of the slice: x: 4, y: 4, z: 8 (z_hi: 4, z_lo: 2; z = z_hi * 2 + z_lo), core: 2. Of those that a mesh axis runs over, the one named last changes fastest.
Arguments:
- field: bfloat16 [2, 1024, 1024, 256], P(None, 'row', 'col'), may hold values from -6 to 6
- phases: float32 [4, 1024, 1024], P(None, 'row', 'col'), may hold values from -3.140625 to 3.140625
- frequencies: float32 [4, 256], replicated, may hold values from 0.5 to 2
- self_mats: bfloat16 [4, 2, 2, 64, 64], replicated, may hold values from -0.375 to 0.375
- cross_mats: bfloat16 [4, 2, 2, 64, 64], replicated, may hold values from -0.375 to 0.375
- plane_mats: bfloat16 [4, 2, 64, 64], replicated, may hold values from -0.5 to 0.5
Outputs:
- result: bfloat16 [2, 1024, 1024, 256], P(None, 'row', 'col')
All inputs are finite; a program needn't handle non-finite values.
Results may differ from a plain program's by a relative error of at most 0.018.
Values may be sent and summed in bfloat16 or wider, within the bound.
A program may use at most 128 MiB of HBM per device.

v0:
```python
import jax
import jax.numpy as jnp
from jax import lax
from jax.sharding import PartitionSpec as P


def for_sending(array):

    def short(part):
        return part.astype(jnp.bfloat16) if part.dtype == jnp.float32 else part

    return jax.tree.map(short, array)


def swapped(block, axis, apart):
    count = lax.axis_size(axis)
    route = []
    for low in range(count):
        high = low | 1 << apart
        if high != low and high < count:
            route += [(low, high), (high, low)]
    return lax.ppermute(block, axis, route)


def pick_half(stack, half_bit):
    return lax.dynamic_index_in_dim(stack, half_bit, 0, keepdims=False)


def axis_product(matrix, part, axis_name):
    if axis_name == "row":
        flat = part.reshape(part.shape[0], part.shape[1] * part.shape[2])
        return jnp.dot(matrix, flat, preferred_element_type=jnp.float32).reshape(part.shape)
    wide = jnp.broadcast_to(matrix, (part.shape[0], matrix.shape[0], matrix.shape[1]))
    return jnp.einsum("rab,rbp->rap", wide, part, preferred_element_type=jnp.float32)


def complex_product(matrix, real_in, imag_in, axis_name):
    real_out = axis_product(matrix[0], real_in, axis_name) - axis_product(
        matrix[1], imag_in, axis_name
    )
    imag_out = axis_product(matrix[0], imag_in, axis_name) + axis_product(
        matrix[1], real_in, axis_name
    )
    return (real_out, imag_out)


def field_swap(parts, axis_name, bit_index):
    if axis_name == "row":
        return jax.tree.map(
            lambda part, own: part.astype(own.dtype),
            swapped(for_sending(parts), "row", bit_index),
            parts,
        )
    return jax.tree.map(
        lambda part, own: part.astype(own.dtype),
        swapped(for_sending(parts), "col", bit_index),
        parts,
    )


def plane_product(plane_level, part):
    points = plane_level.shape[-1]
    shaped = part.reshape(part.shape[0], part.shape[1], part.shape[2] // points, points)
    return jnp.einsum("rcbq,sq->rcbs", shaped, plane_level, preferred_element_type=jnp.float32)


def butterfly_level(
    real_in,
    imag_in,
    angles,
    freq,
    self_level,
    cross_level,
    plane_level,
    axis_name,
    bit_index,
    half_bit,
):
    self_pick = pick_half(self_level, half_bit)
    own_real, own_imag = complex_product(self_pick, real_in, imag_in, axis_name)
    cross_pick = pick_half(cross_level, half_bit)
    near_real, near_imag = field_swap((real_in, imag_in), axis_name, bit_index)
    come_real, come_imag = complex_product(cross_pick, near_real, near_imag, axis_name)
    sum_real = own_real + come_real
    sum_imag = own_imag + come_imag
    theta = angles[:, :, None] * freq[None, None, :]
    cosine = jnp.cos(theta)
    sine = jnp.sin(theta)
    turned_real = (cosine * sum_real - sine * sum_imag).astype(jnp.bfloat16)
    turned_imag = (sine * sum_real + cosine * sum_imag).astype(jnp.bfloat16)
    mixed_real = plane_product(plane_level[0], turned_real) - plane_product(
        plane_level[1], turned_imag
    )
    mixed_imag = plane_product(plane_level[0], turned_imag) + plane_product(
        plane_level[1], turned_real
    )
    return (
        mixed_real.reshape(real_in.shape).astype(jnp.bfloat16),
        mixed_imag.reshape(real_in.shape).astype(jnp.bfloat16),
    )


def local(field, phases, frequencies, self_mats, cross_mats, plane_mats):
    row_top = lax.axis_size("row").bit_length() - 2
    col_top = lax.axis_size("col").bit_length() - 2
    plan = [("row", row_top), ("col", col_top), ("row", 0), ("col", 0)]
    real_part = field[0]
    imag_part = field[1]
    for level in range(len(plan)):
        axis_name, bit_index = plan[level]
        if axis_name == "row":
            half_bit = lax.axis_index("row") >> bit_index & 1
        else:
            half_bit = lax.axis_index("col") >> bit_index & 1
        real_part, imag_part = butterfly_level(
            real_part,
            imag_part,
            phases[level],
            frequencies[level],
            self_mats[level],
            cross_mats[level],
            plane_mats[level],
            axis_name,
            bit_index,
            half_bit,
        )
    return jnp.stack([real_part, imag_part], axis=0)


def solution(mesh):
    return jax.shard_map(
        local,
        mesh=mesh,
        in_specs=(P(None, "row", "col", None), P(None, "row", "col"), P(), P(), P(), P()),
        out_specs=P(None, "row", "col", None),
        check_vma=False,
    )
```

profile of v0, /device:TPU:96, one launch (start us, length us, event | category | flops | bytes accessed | tf_op | source)
XLA Modules:
  0.0 749.8 jit_solution(18009970022850600419)
XLA Ops:
  0.0 5.5 slice_bitcast_fusion.4
  5.6 3.2 collective-permute-start
  11.0 3.3 fusion.106
  19.4 36.5 %collective-permute-done = bf16[64,64,256]{2,1,0:T(8,128)(2,1)} collective-permute-done((bf16[64,64,256]{2,1,0:T(8,128)(2,1)}, bf16[64,64,256]{2,1,0:T(8,128)(2,1)}, u32[]{:S(2)}, u32[]{:S(2)}) %collective-permute-start) | collective-permute-done | bytes 2097184 | tf_op jit(solution)/shard_map/ppermute | solution.py:22
  55.9 3.3 fusion.98
  59.2 40.5 %collective-permute-done.1 = bf16[64,64,256]{2,1,0:T(8,128)(2,1)} collective-permute-done((bf16[64,64,256]{2,1,0:T(8,128)(2,1)}, bf16[64,64,256]{2,1,0:T(8,128)(2,1)}, u32[]{:S(2)}, u32[]{:S(2)}) %collective-permute-start.1) | collective-permute-done | bytes 2097184 | tf_op jit(solution)/shard_map/ppermute | solution.py:22
  99.7 3.3 fusion.94
  103.0 4.0 subtract_add_fusion.3
  107.0 21.8 %fusion.17 = (bf16[64,64,256]{2,0,1:T(8,128)(2,1)S(1)}, bf16[64,64,256]{2,0,1:T(8,128)(2,1)}) fusion(f32[64,64,256]{2,0,1:T(8,128)S(1)} %subtract_add_fusion.3, f32[256]{0:T(256)S(1)} %bitcast.301, f32[64,64]{0,1:T(8,128)S(1)} %copy.26, f32[64,64,256]{2,0,1:T(8,128)S(1)} %fusion.94, bf16[1,2,2,64,64]{4,3,2,1,0:T(8,128)(2,1)S(1)} %get-tuple-element.23, ...), kind=kOutput, calls=%fused_computation.33 | convolution fusion | flops 146800640 | bytes 23118856 | tf_op jit(solution)/shard_map/dot_general | solution.py:32
  128.8 7.1 reshape.199
  136.0 10.1 %fusion.58 = f32[64,64,4,64]{3,1,2,0:T(8,128)} fusion(bf16[64,64,4,64]{3,2,0,1:T(4,128)(2,1)} %reshape.199, bf16[4,2,64,64]{3,2,1,0:T(8,128)(2,1)S(1)} %copy-done.8), kind=kOutput, calls=%fused_computation.83 | convolution fusion | flops 134217728 | bytes 6307840 | tf_op jit(solution)/shard_map/rcbq,sq->rcbs/dot_general | solution.py:64
  146.1 7.7 %fusion.56 = f32[64,64,4,64]{3,1,2,0:T(8,128)} fusion(bf16[64,64,4,64]{3,2,0,1:T(4,128)(2,1)S(1)} %copy-done, bf16[4,2,64,64]{3,2,1,0:T(8,128)(2,1)S(1)} %copy-done.8), kind=kOutput, calls=%fused_computation.81 | convolution fusion | flops 134217728 | bytes 8404992 | tf_op jit(solution)/shard_map/rcbq,sq->rcbs/dot_general | solution.py:64
  153.8 3.7 reshape.198
  157.5 9.5 %add_convert_fusion.3 = bf16[64,64,4,64]{3,1,2,0:T(8,128)(2,1)S(1)} fusion(f32[64,64,4,64]{3,1,2,0:T(8,128)} %fusion.56, bf16[64,64,4,64]{3,2,0,1:T(4,128)(2,1)} %reshape.198, bf16[4,2,64,64]{3,2,1,0:T(8,128)(2,1)S(1)} %copy-done.8), kind=kOutput, calls=%fused_computation.6 | convolution fusion | flops 136314880 | bytes 8404992 | tf_op jit(solution)/shard_map/rcbq,sq->rcbs/dot_general | solution.py:64
  166.9 10.5 %copy.40 = bf16[64,64,4,64]{3,2,1,0:T(4,128)(2,1)} copy(bf16[64,64,4,64]{3,1,2,0:T(8,128)(2,1)S(1)} %add_convert_fusion.3) | data formatting | bytes 4194304 | tf_op jit(solution)/shard_map/convert_element_type | solution.py:99
  177.4 6.0 convert_element_type.99
  183.4 4.6 collective-permute-start.3
  188.0 9.5 %subtract_convert_fusion.3 = bf16[64,64,4,64]{3,1,2,0:T(8,128)(2,1)S(1)} fusion(f32[64,64,4,64]{3,1,2,0:T(8,128)} %fusion.58, bf16[64,64,4,64]{3,2,0,1:T(4,128)(2,1)} %reshape.198, bf16[4,2,64,64]{3,2,1,0:T(8,128)(2,1)S(1)} %copy-done.8), kind=kOutput, calls=%fused_computation.7 | convolution fusion | flops 136314880 | bytes 8404992 | tf_op jit(solution)/shard_map/rcbq,sq->rcbs/dot_general | solution.py:64
  197.5 10.7 %copy.37 = bf16[64,64,4,64]{3,2,1,0:T(4,128)(2,1)} copy(bf16[64,64,4,64]{3,1,2,0:T(8,128)(2,1)S(1)} %subtract_convert_fusion.3) | data formatting | bytes 4194304 | tf_op jit(solution)/shard_map/convert_element_type | solution.py:98
  208.2 6.9 convert_element_type.97
  219.4 55.8 %collective-permute-done.3 = bf16[64,64,256]{2,1,0:T(8,128)(2,1)} collective-permute-done((bf16[64,64,256]{2,1,0:T(8,128)(2,1)S(1)}, bf16[64,64,256]{2,1,0:T(8,128)(2,1)}, u32[]{:S(2)}, u32[]{:S(2)}) %collective-permute-start.3) | collective-permute-done | bytes 2097184 | tf_op jit(solution)/shard_map/ppermute | solution.py:22
  277.4 93.2 %collective-permute-done.2 = bf16[64,64,256]{2,1,0:T(8,128)(2,1)S(1)} collective-permute-done((bf16[64,64,256]{2,1,0:T(8,128)(2,1)}, bf16[64,64,256]{2,1,0:T(8,128)(2,1)S(1)}, u32[]{:S(2)}, u32[]{:S(2)}) %collective-permute-start.2) | collective-permute-done | bytes 2097184 | tf_op jit(solution)/shard_map/ppermute | solution.py:22
  372.4 19.9 %fusion.21 = (bf16[64,64,256]{2,1,0:T(8,128)(2,1)S(1)}, bf16[64,64,256]{2,1,0:T(8,128)(2,1)}) fusion(f32[64,64,256]{2,1,0:T(8,128)S(1)} %subtract_add_fusion.2, f32[256]{0:T(256)S(1)} %bitcast.299, f32[64,64]{1,0:T(8,128)S(1)} %get-tuple-element.28, f32[64,64,256]{2,1,0:T(8,128)S(1)} %fusion.134, bf16[64,64,256]{2,1,0:T(8,128)(2,1)} %collective-permute-done.3, ...), kind=kOutput, calls=%fused_computation.37 | convolution fusion | flops 146800640 | bytes 23094272 | tf_op jit(solution)/shard_map/rab,rbp->rap/dot_general | solution.py:34
  392.3 7.1 reshape.201
  399.4 6.8 fusion.48
  406.2 4.5 fusion.50
  410.7 3.3 reshape.200
  414.0 5.9 subtract_convert_fusion.2
  419.9 10.3 %copy.43 = bf16[64,64,4,64]{3,2,1,0:T(4,128)(2,1)} copy(bf16[64,64,4,64]{3,1,2,0:T(8,128)(2,1)S(1)} %subtract_convert_fusion.2) | data formatting | bytes 4194304 | tf_op jit(solution)/shard_map/convert_element_type | solution.py:98
  430.2 6.9 convert_element_type.106
  437.4 5.9 add_convert_fusion.2
  443.3 10.3 %copy.47 = bf16[64,64,4,64]{3,2,1,0:T(4,128)(2,1)} copy(bf16[64,64,4,64]{3,1,2,0:T(8,128)(2,1)S(1)} %add_convert_fusion.2) | data formatting | bytes 4194304 | tf_op jit(solution)/shard_map/convert_element_type | solution.py:99
  453.6 6.9 convert_element_type.107
  461.5 6.0 convert_element_type.105
  467.5 5.0 convert_element_type.103
  472.5 2.4 fusion.88
  477.0 3.3 fusion.84
  480.3 3.3 fusion.80
  483.6 4.0 subtract_add_fusion.1
  487.6 21.6 %fusion.25 = (bf16[64,64,256]{2,0,1:T(8,128)(2,1)S(1)}, bf16[64,64,256]{2,0,1:T(8,128)(2,1)}) fusion(f32[64,64,256]{2,0,1:T(8,128)S(1)} %subtract_add_fusion.1, f32[256]{0:T(256)S(1)} %bitcast.300, f32[64,64]{0,1:T(8,128)S(1)} %copy.25, f32[64,64,256]{2,0,1:T(8,128)S(1)} %fusion.80, bf16[1,2,2,64,64]{4,3,2,1,0:T(8,128)(2,1)S(1)} %get-tuple-element.24, ...), kind=kOutput, calls=%fused_computation.41 | convolution fusion | flops 146800640 | bytes 23118856 | tf_op jit(solution)/shard_map/dot_general | solution.py:32
  509.2 7.2 reshape.205
  516.4 10.1 %fusion.42 = f32[64,64,4,64]{3,1,2,0:T(8,128)} fusion(bf16[64,64,4,64]{3,2,0,1:T(4,128)(2,1)} %reshape.205, bf16[4,2,64,64]{3,2,1,0:T(8,128)(2,1)S(1)} %copy-done.8), kind=kOutput, calls=%fused_computation.67 | convolution fusion | flops 134217728 | bytes 6307840 | tf_op jit(solution)/shard_map/rcbq,sq->rcbs/dot_general | solution.py:64
  526.5 7.7 %fusion.40 = f32[64,64,4,64]{3,1,2,0:T(8,128)} fusion(bf16[64,64,4,64]{3,2,0,1:T(4,128)(2,1)S(1)} %copy-done.2, bf16[4,2,64,64]{3,2,1,0:T(8,128)(2,1)S(1)} %copy-done.8), kind=kOutput, calls=%fused_computation.65 | convolution fusion | flops 134217728 | bytes 8404992 | tf_op jit(solution)/shard_map/rcbq,sq->rcbs/dot_general | solution.py:64
  534.3 3.4 reshape.204
  537.6 9.5 %add_convert_fusion.1 = bf16[64,64,4,64]{3,1,2,0:T(8,128)(2,1)S(1)} fusion(f32[64,64,4,64]{3,1,2,0:T(8,128)} %fusion.40, bf16[64,64,4,64]{3,2,0,1:T(4,128)(2,1)} %reshape.204, bf16[4,2,64,64]{3,2,1,0:T(8,128)(2,1)S(1)} %copy-done.8), kind=kOutput, calls=%fused_computation.2 | convolution fusion | flops 136314880 | bytes 8404992 | tf_op jit(solution)/shard_map/rcbq,sq->rcbs/dot_general | solution.py:64
  547.1 10.8 %copy.62 = bf16[64,64,4,64]{3,2,1,0:T(4,128)(2,1)} copy(bf16[64,64,4,64]{3,1,2,0:T(8,128)(2,1)S(1)} %add_convert_fusion.1) | data formatting | bytes 4194304 | tf_op jit(solution)/shard_map/convert_element_type | solution.py:99
  557.9 6.0 convert_element_type.113
  565.4 9.5 %subtract_convert_fusion.1 = bf16[64,64,4,64]{3,1,2,0:T(8,128)(2,1)S(1)} fusion(f32[64,64,4,64]{3,1,2,0:T(8,128)} %fusion.42, bf16[64,64,4,64]{3,2,0,1:T(4,128)(2,1)} %reshape.204, bf16[4,2,64,64]{3,2,1,0:T(8,128)(2,1)S(1)} %copy-done.8), kind=kOutput, calls=%fused_computation.3 | convolution fusion | flops 136314880 | bytes 8404992 | tf_op jit(solution)/shard_map/rcbq,sq->rcbs/dot_general | solution.py:64
  574.9 10.5 %copy.59 = bf16[64,64,4,64]{3,2,1,0:T(4,128)(2,1)} copy(bf16[64,64,4,64]{3,1,2,0:T(8,128)(2,1)S(1)} %subtract_convert_fusion.1) | data formatting | bytes 4194304 | tf_op jit(solution)/shard_map/convert_element_type | solution.py:98
  585.4 7.0 convert_element_type.111
  596.1 16.5 %collective-permute-done.7 = bf16[64,64,256]{2,1,0:T(8,128)(2,1)} collective-permute-done((bf16[64,64,256]{2,1,0:T(8,128)(2,1)S(1)}, bf16[64,64,256]{2,1,0:T(8,128)(2,1)}, u32[]{:S(2)}, u32[]{:S(2)}) %collective-permute-start.7) | collective-permute-done | bytes 2097184 | tf_op jit(solution)/shard_map/ppermute | solution.py:22
  614.8 41.6 %collective-permute-done.6 = bf16[64,64,256]{2,1,0:T(8,128)(2,1)S(1)} collective-permute-done((bf16[64,64,256]{2,1,0:T(8,128)(2,1)}, bf16[64,64,256]{2,1,0:T(8,128)(2,1)S(1)}, u32[]{:S(2)}, u32[]{:S(2)}) %collective-permute-start.6) | collective-permute-done | bytes 2097184 | tf_op jit(solution)/shard_map/ppermute | solution.py:22
  658.3 19.9 %fusion.29 = (bf16[64,64,256]{2,1,0:T(8,128)(2,1)S(1)}, bf16[64,64,256]{2,1,0:T(8,128)(2,1)}) fusion(f32[64,64,256]{2,1,0:T(8,128)S(1)} %subtract_add_fusion, f32[256]{0:T(256)S(1)} %bitcast.298, f32[64,64]{1,0:T(8,128)S(1)} %copy-done.12, f32[64,64,256]{2,1,0:T(8,128)S(1)} %fusion.124, bf16[64,64,256]{2,1,0:T(8,128)(2,1)} %collective-permute-done.7, ...), kind=kOutput, calls=%fused_computation.45 | convolution fusion | flops 146800640 | bytes 23094272 | tf_op jit(solution)/shard_map/rab,rbp->rap/dot_general | solution.py:34
  678.2 7.1 reshape.207
  685.3 6.8 fusion.34
  692.1 4.5 fusion.32
  696.6 3.4 reshape.206
  700.0 5.9 subtract_convert_fusion
  705.9 10.3 %copy.65 = bf16[64,64,4,64]{3,2,1,0:T(4,128)(2,1)} copy(bf16[64,64,4,64]{3,1,2,0:T(8,128)(2,1)S(1)} %subtract_convert_fusion) | data formatting | bytes 4194304 | tf_op jit(solution)/shard_map/convert_element_type | solution.py:98
  716.2 6.4 convert_element_type.117
  722.5 5.9 add_convert_fusion
  728.5 10.3 %copy.68 = bf16[64,64,4,64]{3,2,1,0:T(4,128)(2,1)} copy(bf16[64,64,4,64]{3,1,2,0:T(8,128)(2,1)S(1)} %add_convert_fusion) | data formatting | bytes 4194304 | tf_op jit(solution)/shard_map/convert_element_type | solution.py:99
  738.8 6.9 convert_element_type.119
  745.7 4.0 pad_maximum_fusion
  (69 shorter events, 28.3 us)
Async XLA Ops:
  0.0 9.1 %copy-start.9 = (bf16[4,2,2,64,64]{4,3,2,1,0:T(8,128)(2,1)S(1)}, bf16[4,2,2,64,64]{4,3,2,1,0:T(8,128)(2,1)}, u32[]{:S(2)}) copy-start(bf16[4,2,2,64,64]{4,3,2,1,0:T(8,128)(2,1)} %param.9) | copy-start | bytes 393220
  0.0 9.1 %copy-start.13 = (f32[4,64,64]{2,1,0:T(8,128)S(1)}, f32[4,64,64]{2,1,0:T(8,128)}, u32[]{:S(2)}) copy-start(f32[4,64,64]{2,1,0:T(8,128)} %param.7) | copy-start | bytes 196612
  0.0 9.8 %copy-start.10 = (bf16[4,2,2,64,64]{4,3,2,1,0:T(8,128)(2,1)S(1)}, bf16[4,2,2,64,64]{4,3,2,1,0:T(8,128)(2,1)}, u32[]{:S(2)}) copy-start(bf16[4,2,2,64,64]{4,3,2,1,0:T(8,128)(2,1)} %param.10) | copy-start | bytes 393220
  0.0 10.5 %copy-start.15 = (f32[4,256]{1,0:T(4,128)S(1)}, f32[4,256]{1,0:T(4,128)}, u32[]{:S(2)}) copy-start(f32[4,256]{1,0:T(4,128)} %param.8) | copy-start | bytes 12292
  5.6 50.3 %collective-permute-start = (bf16[64,64,256]{2,1,0:T(8,128)(2,1)}, bf16[64,64,256]{2,1,0:T(8,128)(2,1)}, u32[]{:S(2)}, u32[]{:S(2)}) collective-permute-start(bf16[64,64,256]{2,1,0:T(8,128)(2,1)} %get-tuple-element.14), channel_id=1, source_target_pairs={{0,128},{128,0},{16,144},{144,16},{32,160},{160,32},{48,176},{176,... | collective-permute-start | bytes 6291464 | tf_op jit(solution)/shard_map/ppermute | solution.py:22
  8.8 90.9 %collective-permute-start.1 = (bf16[64,64,256]{2,1,0:T(8,128)(2,1)}, bf16[64,64,256]{2,1,0:T(8,128)(2,1)}, u32[]{:S(2)}, u32[]{:S(2)}) collective-permute-start(bf16[64,64,256]{2,1,0:T(8,128)(2,1)} %get-tuple-element.13), channel_id=1, source_target_pairs={{0,128},{128,0},{16,144},{144,16},{32,160},{160,32},{48,176},{176,... | collective-permute-start | bytes 6291464 | tf_op jit(solution)/shard_map/ppermute | solution.py:22
  9.8 4.5 copy-start.7
  128.8 7.1 copy-start.8
  136.0 10.1 %copy-start = (bf16[64,64,4,64]{3,2,0,1:T(4,128)(2,1)S(1)}, bf16[64,64,4,64]{3,2,0,1:T(4,128)(2,1)}, u32[]{:S(2)}) copy-start(bf16[64,64,4,64]{3,2,0,1:T(4,128)(2,1)} %reshape.199) | copy-start | bytes 6291460
  183.4 91.7 %collective-permute-start.3 = (bf16[64,64,256]{2,1,0:T(8,128)(2,1)S(1)}, bf16[64,64,256]{2,1,0:T(8,128)(2,1)}, u32[]{:S(2)}, u32[]{:S(2)}) collective-permute-start(bf16[64,64,256]{2,1,0:T(8,128)(2,1)S(1)} %convert_element_type.99), channel_id=1, source_target_pairs={{0,8},{8,0},{1,9},{9,1},{2,10},{10,2},{3,11},{11,3},{4,12},{12,4},... | collective-permute-start | bytes 6291464 | tf_op jit(solution)/shard_map/ppermute | solution.py:22
  215.1 2.2 copy-start.4
  215.1 155.4 %collective-permute-start.2 = (bf16[64,64,256]{2,1,0:T(8,128)(2,1)}, bf16[64,64,256]{2,1,0:T(8,128)(2,1)S(1)}, u32[]{:S(2)}, u32[]{:S(2)}) collective-permute-start(bf16[64,64,256]{2,1,0:T(8,128)(2,1)} %convert_element_type.97), channel_id=1, source_target_pairs={{0,8},{8,0},{1,9},{9,1},{2,10},{10,2},{3,11},{11,3},{4,12},{12,4},... | collective-permute-start | bytes 6291464 | tf_op jit(solution)/shard_map/ppermute | solution.py:22
  399.4 6.8 copy-start.1
  437.2 39.8 %collective-permute-start.4 = (bf16[64,64,256]{2,1,0:T(8,128)(2,1)}, bf16[64,64,256]{2,1,0:T(8,128)(2,1)}, u32[]{:S(2)}, u32[]{:S(2)}) collective-permute-start(bf16[64,64,256]{2,1,0:T(8,128)(2,1)} %convert_element_type.106), channel_id=1, source_target_pairs={{0,16},{16,0},{32,48},{48,32},{64,80},{80,64},{96,112},{112,96},{1... | collective-permute-start | bytes 6291464 | tf_op jit(solution)/shard_map/ppermute | solution.py:22
  460.6 19.8 %collective-permute-start.5 = (bf16[64,64,256]{2,1,0:T(8,128)(2,1)}, bf16[64,64,256]{2,1,0:T(8,128)(2,1)}, u32[]{:S(2)}, u32[]{:S(2)}) collective-permute-start(bf16[64,64,256]{2,1,0:T(8,128)(2,1)} %convert_element_type.107), channel_id=1, source_target_pairs={{0,16},{16,0},{32,48},{48,32},{64,80},{80,64},{96,112},{112,96},{1... | collective-permute-start | bytes 6291464 | tf_op jit(solution)/shard_map/ppermute | solution.py:22
  472.5 2.5 copy-start.6
  516.4 10.1 %copy-start.2 = (bf16[64,64,4,64]{3,2,0,1:T(4,128)(2,1)S(1)}, bf16[64,64,4,64]{3,2,0,1:T(4,128)(2,1)}, u32[]{:S(2)}) copy-start(bf16[64,64,4,64]{3,2,0,1:T(4,128)(2,1)} %reshape.205) | copy-start | bytes 6291460
  563.9 48.7 %collective-permute-start.7 = (bf16[64,64,256]{2,1,0:T(8,128)(2,1)S(1)}, bf16[64,64,256]{2,1,0:T(8,128)(2,1)}, u32[]{:S(2)}, u32[]{:S(2)}) collective-permute-start(bf16[64,64,256]{2,1,0:T(8,128)(2,1)S(1)} %convert_element_type.113), channel_id=1, source_target_pairs={{0,1},{1,0},{2,3},{3,2},{4,5},{5,4},{6,7},{7,6},{8,9},{9,8},{10,11... | collective-permute-start | bytes 6291464 | tf_op jit(solution)/shard_map/ppermute | solution.py:22
  585.4 7.5 %copy-start.11 = (bf16[1,2,2,64,64]{4,3,2,1,0:T(8,128)(2,1)S(1)}, bf16[1,2,2,64,64]{4,3,2,1,0:T(8,128)(2,1)}, u32[]{:S(2)}) copy-start(bf16[1,2,2,64,64]{4,3,2,1,0:T(8,128)(2,1)} %get-tuple-element.21) | copy-start | bytes 98308
  592.4 1.6 copy-start.5
  592.4 64.0 %collective-permute-start.6 = (bf16[64,64,256]{2,1,0:T(8,128)(2,1)}, bf16[64,64,256]{2,1,0:T(8,128)(2,1)S(1)}, u32[]{:S(2)}, u32[]{:S(2)}) collective-permute-start(bf16[64,64,256]{2,1,0:T(8,128)(2,1)} %convert_element_type.111), channel_id=1, source_target_pairs={{0,1},{1,0},{2,3},{3,2},{4,5},{5,4},{6,7},{7,6},{8,9},{9,8},{10,11... | collective-permute-start | bytes 6291464 | tf_op jit(solution)/shard_map/ppermute | solution.py:22
  657.1 1.2 copy-start.12
  657.1 1.2 copy-start.14
  685.3 6.8 copy-start.3
where the time goes:
time: 760 us; the launch traced here: 750 us
  waiting for transfers between devices  284 us (37%)
  matrix products  251 us (33%)
  local copies, waits for them, and re-layouts  198 us (26%)
  starting transfers between devices  12.7 us (2%)
    ppermute x8, waiting for transfers between devices, swapped(): return lax.ppermute(block, axis, route)  284 us
    dot_general x16, matrix products, plane_product(): jnp.einsum('rcbq,sq->rcbs', shaped, plane_level, preferred_element_type=j...  120 us
    dot_general x16, matrix products, axis_product(): jnp.dot(matrix, flat, preferred_element_type=jnp.float32)  77.5 us
    convert_element_type x9, local copies, waits for them, and re-layouts, butterfly_level(): mixed_real.reshape(real_in.shape).astype(jnp.bfloat16)  74 us
    convert_element_type x9, local copies, waits for them, and re-layouts, butterfly_level(): mixed_imag.reshape(real_in.shape).astype(jnp.bfloat16)  73.7 us
    dot_general x16, matrix products, axis_product(): jnp.einsum('rab,rbp->rap', wide, part, preferred_element_type=jnp.float32)  53.4 us
    reshape x8, local copies, waits for them, and re-layouts, plane_product(): part.reshape(part.shape[0], part.shape[1], part.shape[2] // points, points)  42.2 us
  transfers between devices with their start and end apart: 8, of which 6 were waited for; matrix products, arithmetic and copies ran while one was open for 16% of the time, Pallas kernels for 0%

commit v1 on v0

v1 whole, which is shorter than its diff:
```python
import functools

import jax
import jax.numpy as jnp
from jax import lax
from jax.experimental import pallas as pl
from jax.experimental.pallas import tpu as pltpu
from jax.sharding import PartitionSpec as P

MESH = pl.DeviceIdType.MESH
F32 = jnp.float32
BF16 = jnp.bfloat16
R = 64
N = 8
Q = R // N
W = 3
SINE = (
    6.283182621002197,
    -41.34142303466797,
    81.59618377685547,
    -76.5801010131836,
    41.20539093017578,
    -12.27125358581543,
)


def kernel(
    x, phases, freqs, selfs, crosses, planes, out,
    stage, a, s, y, f, g, b2s, b2r, b3s, b3r, zb, tab, ostage, zphase, mats, mixes,
    in_sem, ph_s, ph_r, zf_s, zf_r, y_s, y_r, c_s, c_r, x_s, x_r, zb_s, zb_r, out_sem,
):
    gr, gc = lax.axis_index("row"), lax.axis_index("col")
    nr, nc = lax.axis_size("row"), lax.axis_size("col")
    half = (gr // (nr // 2), gc // (nc // 2), gr % 2, gc % 2)
    to_y = (gr + nr // 2 - nr * half[0], gc)
    to_z = (gr, gc + nc // 2 - nc * half[1])
    to_c = (gr + 1 - 2 * half[2], gc)
    to_x = (gr, gc + 1 - 2 * half[3])

    def lanes_of(which):
        return pl.ds(pl.multiple_of(which * 2 * R, 2 * R), 2 * R)

    mine, theirs = lanes_of(half[1]), lanes_of(1 - half[1])

    def load_copy(n, side, lanes):
        return pltpu.make_async_copy(
            x.at[:, :, pl.ds(pl.multiple_of(n * 16, 16), 16), lanes],
            stage.at[side * 4 + n], in_sem.at[side * 4 + n])

    def remote(src, dst, ssem, rsem, to):
        return pltpu.make_async_remote_copy(
            src_ref=src, dst_ref=dst, send_sem=ssem, recv_sem=rsem,
            device_id=to, device_id_type=MESH)

    def phase_copy():
        return remote(phases, zphase, ph_s, ph_r, to_z)

    def z_fwd(i):
        return remote(s.at[i], a.at[1, i], zf_s.at[i], zf_r.at[i], to_z)

    def y_copy(grp, i):
        n = grp * 2 * N + i
        return remote(a.at[grp, i], y.at[grp, i], y_s.at[n], y_r.at[n], to_y)

    def c_copy(grp, u, j):
        n = grp * 2 * N + u * N + j
        return remote(b2s.at[grp, j], b2r.at[grp, u * N + j], c_s.at[n], c_r.at[n], to_c)

    def x_copy(grp, u, j):
        n = grp * 2 * N + u * N + j
        return remote(b3s.at[grp, j], b3r.at[grp, u * N + j], x_s.at[n], x_r.at[n], to_x)

    def z_back(i):
        return remote(s.at[i], zb.at[i], zb_s.at[i], zb_r.at[i], to_z)

    def out_copy(side, j, lanes):
        return pltpu.make_async_copy(
            ostage.at[side * N + j],
            out.at[:, pl.ds(pl.multiple_of(j * Q, Q), Q), :, lanes],
            out_sem.at[side * N + j])

    def loop(n, body):
        lax.fori_loop(0, n, lambda i, c: (body(i), c)[1], 0)

    for n in range(4):
        load_copy(n, 0, theirs).start()
    for n in range(4):
        load_copy(n, 1, mine).start()

    barrier = pltpu.get_barrier_semaphore()
    for to in (to_y, to_z, to_c, to_x):
        pl.semaphore_signal(barrier, inc=1, device_id=to, device_id_type=MESH)
    pl.semaphore_wait(barrier, 4)
    phase_copy().start()

    lane = lax.broadcasted_iota(jnp.int32, (R, 2 * R), 1)
    low = lane < R

    def turn(v):
        return pltpu.roll(v, R, 1)

    def pack(n, side, put):
        f[0, pl.ds(0, R * 16)] = stage[side * 4 + n, 0].reshape(R * 16, 2 * R).astype(F32)
        f[1, pl.ds(0, R * 16)] = stage[side * 4 + n, 1].reshape(R * 16, 2 * R).astype(F32)
        for k in range(16):
            re = f[0, pl.ds(k, R, stride=16)]
            im = f[1, pl.ds(k, R, stride=16)]
            put(n * 2 + k // Q, k % Q,
                jnp.where(low, re, turn(im)).astype(BF16),
                jnp.where(low, turn(re), im).astype(BF16))

    def put_s(j, k, first, second):
        s[j, k] = first
        s[N + j, k] = second

    def put_a(j, k, first, second):
        a[0, j, k] = first
        a[0, N + j, k] = second

    def pack_theirs(n):
        load_copy(n, 0, theirs).wait()
        pack(n, 0, put_s)

    def pack_mine(n):
        load_copy(n, 1, mine).wait()
        pack(n, 1, put_a)
        y_copy(0, 2 * n).start()
        y_copy(0, 2 * n + 1).start()

    pack_theirs(0)
    z_fwd(0).start()
    z_fwd(1).start()
    pack_theirs(1)
    z_fwd(2).start()
    loop(2, lambda n: pack_theirs(n + 2))
    loop(4, pack_mine)

    for k in range(4):
        h = half[k]
        own = selfs[k, h]
        far = crosses[k, h]
        if k == 1:
            own2 = selfs[k, 1 - h]
            far2 = crosses[k, 1 - h]
            rows = [(own, far), (far2, own2)]
        else:
            rows = [(own, far)]
        blocks = []
        for left, right in rows:
            for part in range(2):
                blocks.append(jnp.concatenate(
                    [left[part].astype(F32), right[part].astype(F32)], axis=1))
        m = jnp.concatenate(blocks, axis=0)
        mats[k, pl.ds(0, m.shape[0])] = m.astype(BF16)
        re, im = planes[k, 0].astype(F32), planes[k, 1].astype(F32)
        wide = jnp.concatenate([
            jnp.concatenate([re, -im, -im, -re], axis=1),
            jnp.concatenate([im, re, re, -im], axis=1)], axis=0)
        mixes[k] = wide.T.astype(BF16)

    sub = lax.broadcasted_iota(jnp.int32, (R, R), 0)
    col = lax.broadcasted_iota(jnp.int32, (R, R), 1)
    quarter = jnp.where(low, 0.0, 0.25)

    def table(k, grp, j):
        ph = phases if grp == 0 else zphase
        fr = freqs[pl.ds(k, 1), mine] * (0.5 / jnp.pi)
        low1 = lax.broadcasted_iota(jnp.int32, (1, 2 * R), 1) < R
        frs = (jnp.where(low1, fr, turn(fr)), jnp.where(low1, turn(fr), fr))

        def one(q):
            o = j * Q + q
            if k % 2 == 0:
                picked = jnp.where(col == o, ph[k], 0.0)
            else:
                picked = jnp.where(col == sub, ph[k, pl.ds(o, 1)], 0.0)
            angle = jnp.sum(picked, axis=1, keepdims=True)
            for u in range(2):
                t = angle * frs[u] + quarter
                t = t - jnp.round(t)
                t2 = t * t
                p = SINE[5]
                for c in SINE[4::-1]:
                    p = p * t2 + c
                tab[k, grp, u * N + j, q] = (p * t).astype(BF16)

        for q in range(Q):
            one(q)

    def rotate(k, grp, i, q, p_, q_):
        t = tab[k, grp, i, q].astype(F32)
        r = turn(t)
        sine = jnp.where(low, t, r)
        cosine = jnp.where(low, r, t)
        return jnp.concatenate(
            [(cosine * p_ - sine * q_).astype(BF16), (sine * p_ + cosine * q_).astype(BF16)],
            axis=1)

    def mix(k, rows):
        return jnp.dot(jnp.concatenate(rows, axis=0), mixes[k], preferred_element_type=F32)

    def apart(k, grp, i, own, far, put):
        m = mats[k, pl.ds(0, 2 * R)]
        for q in range(0, Q, 2):
            v = [jnp.concatenate([own[q + d], far[q + d]], axis=0) for d in range(2)]
            pq = jnp.dot(m, jnp.concatenate(v, axis=1), preferred_element_type=F32)
            rows = [
                rotate(k, grp, i, q + d, pq[:R, d * 2 * R:(d + 1) * 2 * R],
                       pq[R:, d * 2 * R:(d + 1) * 2 * R])
                for d in range(2)]
            v = mix(k, rows)
            for d in range(2):
                put(q + d, v[d * R:(d + 1) * R])

    def row_of(o):
        return pl.ds(pl.multiple_of(o * R, R), R)

    def put_f(grp, j):
        def put(q, v):
            f[grp, row_of(j * Q + q)] = v
        return put

    def level0(grp, u, j):
        i = u * N + j
        y_copy(grp, i).wait()
        apart(0, grp, i, a.at[grp, i], y.at[grp, i], put_f(grp, j))

    def level1(u, j):
        m = mats[1]
        for q in range(0, Q, 2):
            v = []
            for d in range(2):
                o = j * Q + q + d
                v.append(jnp.concatenate(
                    [f[grp, pl.ds(o, R, stride=R)].astype(BF16) for grp in range(2)], axis=0))
            pq = jnp.dot(m, jnp.concatenate(v, axis=1), preferred_element_type=F32)
            for grp in range(2):
                rows = [
                    rotate(1, grp, u * N + j, q + d,
                           pq[grp * 2 * R:grp * 2 * R + R, d * 2 * R:(d + 1) * 2 * R],
                           pq[grp * 2 * R + R:(grp + 1) * 2 * R, d * 2 * R:(d + 1) * 2 * R])
                    for d in range(2)]
                w = mix(1, rows)
                for d in range(2):
                    g[grp, row_of(j * Q + q + d)] = w[d * R:(d + 1) * R]

    def core_send(u, j):
        for grp in range(2):
            for q in range(Q):
                b2s[grp, j, q] = g[grp, pl.ds(j * Q + q, R, stride=R)].astype(BF16)
            c_copy(grp, u, j).start()

    def level2(u, j):
        for grp in range(2):
            c_copy(grp, u, j).wait()
            apart(2, grp, u * N + j, b2s.at[grp, j], b2r.at[grp, u * N + j], put_f(grp, j))

    def x_pack(grp, j):
        for q in range(Q):
            b3s[grp, j, q] = f[grp, pl.ds(j * Q + q, R, stride=R)].astype(BF16)

    def x_send(u, j):
        x_pack(1, j)
        x_copy(1, u, j).start()
        x_pack(0, j)

    def level3(grp, u, j):
        i = u * N + j
        dst = a.at[0, i] if grp == 0 else s.at[i]

        def put(q, v):
            dst[q] = v.astype(BF16)

        x_copy(grp, u, j).wait()
        apart(3, grp, i, b3s.at[grp, j], b3r.at[grp, i], put)

    def merge(first, second, side, j, lanes):
        for q in range(Q):
            p0, p1 = first[q].astype(F32), second[q].astype(F32)
            ostage[side * N + j, 0, q] = jnp.where(low, p0, turn(p1)).astype(BF16)
            ostage[side * N + j, 1, q] = jnp.where(low, turn(p0), p1).astype(BF16)
        out_copy(side, j, lanes).start()

    def z_arrive(i, more):
        z_fwd(i).wait()
        if more:
            z_fwd(i + W).start()
        y_copy(1, i).start()

    phase_copy().wait()

    def come0(j):
        for k in range(4):
            table(k, 0, j)
            table(k, 1, j)
        level0(0, 0, j)
        z_arrive(j, True)

    come0(0)

    def come(j):
        come0(j + 1)
        level0(1, 0, j)

    loop(N - 1, come)
    loop(N, lambda j: y_copy(0, N + j).start())
    level0(1, 0, N - 1)

    loop(N // 2, lambda j: level1(0, j))
    z_arrive(N, True)
    loop(N // 2, lambda j: level1(0, j + N // 2))
    z_arrive(N + 1, True)
    loop(N, lambda j: core_send(0, j))
    loop(N, lambda j: level2(0, j))
    z_arrive(N + 2, True)
    loop(N, lambda j: x_send(0, j))
    z_arrive(N + 3, True)
    loop(N, lambda j: level0(0, 1, j))

    def come1(j):
        z_arrive(N + 4 + j, False)
        level0(1, 1, j)
        for d in range(2):
            level3(1, 0, 2 * j + d)
            x_copy(0, 0, 2 * j + d).start()

    z_arrive(N + 4, True)
    level0(1, 1, 0)
    level3(1, 0, 0)
    x_copy(0, 0, 0).start()
    level3(1, 0, 1)
    x_copy(0, 0, 1).start()
    loop(1, lambda _: come1(1))
    z_back(0).start()
    loop(1, lambda _: come1(2))
    z_back(1).start()
    loop(1, lambda _: come1(3))
    loop(N - 2, lambda j: z_back(j + 2).start())
    loop(N - 4, lambda j: level0(1, 1, j + 4))

    loop(N, lambda j: level1(1, j))
    loop(N, lambda j: core_send(1, j))
    loop(N, lambda j: level2(1, j))
    loop(N, lambda j: level3(0, 0, j))
    loop(N, lambda j: x_send(1, j))

    def back1(j):
        level3(1, 1, j)
        z_back(N + j).start()
        x_copy(0, 1, j).start()

    loop(N, back1)

    def own1(j):
        level3(0, 1, j)
        merge(a.at[0, j], a.at[0, N + j], 0, j, mine)

    loop(N, own1)

    def last(j):
        z_back(j).wait()
        z_back(N + j).wait()
        merge(zb.at[j], zb.at[N + j], 1, j, theirs)

    loop(N, last)
    loop(N, lambda j: out_copy(0, j, mine).wait())
    loop(N, lambda j: out_copy(1, j, theirs).wait())


def local(field, phases, frequencies, self_mats, cross_mats, plane_mats):
    vm = pl.BlockSpec(memory_space=pltpu.VMEM)
    anywhere = pl.BlockSpec(memory_space=pl.ANY)
    chunk = (Q, R, 2 * R)
    unit2 = (2 * N,) + chunk
    dma = pltpu.SemaphoreType.DMA
    return pl.pallas_call(
        kernel,
        out_shape=jax.ShapeDtypeStruct(field.shape, field.dtype),
        in_specs=[anywhere, vm, vm, vm, vm, vm],
        out_specs=anywhere,
        scratch_shapes=[
            pltpu.VMEM((8, 2, R, 16, 2 * R), BF16),
            pltpu.VMEM((2,) + unit2, BF16),
            pltpu.VMEM(unit2, BF16),
            pltpu.VMEM((2,) + unit2, BF16),
            pltpu.VMEM((2, R * R, 2 * R), F32),
            pltpu.VMEM((2, R * R, 2 * R), F32),
            pltpu.VMEM((2, N) + chunk, BF16),
            pltpu.VMEM((2,) + unit2, BF16),
            pltpu.VMEM((2, N) + chunk, BF16),
            pltpu.VMEM((2,) + unit2, BF16),
            pltpu.VMEM(unit2, BF16),
            pltpu.VMEM((4, 2) + unit2, BF16),
            pltpu.VMEM((2 * N, 2) + chunk, BF16),
            pltpu.VMEM((4, R, R), F32),
            pltpu.VMEM((4, 4 * R, 2 * R), BF16),
            pltpu.VMEM((4, 4 * R, 2 * R), BF16),
            dma((8,)), dma, dma, dma((2 * N,)), dma((2 * N,)),
            dma((4 * N,)), dma((4 * N,)), dma((4 * N,)), dma((4 * N,)),
            dma((4 * N,)), dma((4 * N,)), dma((2 * N,)), dma((2 * N,)), dma((2 * N,)),
        ],
        compiler_params=pltpu.CompilerParams(
            collective_id=0, has_side_effects=True, vmem_limit_bytes=62 * 2**20),
        cost_estimate=pl.CostEstimate(
            flops=12 * 2**30, bytes_accessed=2**23, transcendentals=2**23),
    )(field, phases, frequencies, self_mats, cross_mats, plane_mats)


def solution(mesh):
    return jax.shard_map(
        local,
        mesh=mesh,
        in_specs=(P(None, "row", "col", None), P(None, "row", "col"), P(), P(), P(), P()),
        out_specs=P(None, "row", "col", None),
        check_vma=False,
    )
```

time: 760 us -> 209 us (0.28)
  waiting for transfers between devices: 284 us -> 0 us
  matrix products: 251 us -> 0 us
  Pallas kernels: 0 us -> 200 us
  local copies, waits for them, and re-layouts: 198 us -> 4.79 us
  starting transfers between devices: 12.7 us -> 0 us
    ppermute x8 -> x0, waiting for transfers between devices: 284 us -> none  [swapped(): return lax.ppermute(block, axis, route)]
    dot_general x48 -> x0, matrix products: 251 us -> none  [the longest x16 120 us: plane_product(): jnp.einsum('rcbq,sq->rcbs', shaped, plane_level, preferred_element_type=j...]
    pallas_call x0 -> x1, Pallas kernels: none -> 200 us  [local(): pl.pallas_call(kernel, out_shape=jax.ShapeDtypeStruct(field.shape, field....]
    convert_element_type x18 -> x0, local copies, waits for them, and re-layouts: 148 us -> none  [the longest x9 74 us: butterfly_level(): mixed_real.reshape(real_in.shape).astype(jnp.bfloat16)]
    reshape x8 -> x0, local copies, waits for them, and re-layouts: 42.2 us -> none  [plane_product(): part.reshape(part.shape[0], part.shape[1], part.shape[2] // points, points)]
    ppermute x8 -> x0, starting transfers between devices: 12.7 us -> none  [swapped(): return lax.ppermute(block, axis, route)]
  transfers between devices with their start and end apart: 8 -> 0, of which waited for: 6 -> 0; matrix products, arithmetic and copies ran while one was open for 16% -> 0% of each run, Pallas kernels for 0% -> 0%
where the time goes in v1:
time: 209 us; the launch traced here: 205 us
  Pallas kernels  200 us (96%)
  local copies, waits for them, and re-layouts  4.79 us (2%)
    pallas_call x1, Pallas kernels, local(): pl.pallas_call(kernel, out_shape=jax.ShapeDtypeStruct(field.shape, field....  200 us
    unnamed x1, local copies, waits for them, and re-layouts  4.79 us

profile of v1, /device:TPU:96, one launch (start us, length us, event | category | flops | bytes accessed | tf_op | source)
XLA Modules:
  0.0 205.0 jit_solution(8885502281510167812)
XLA Ops:
  0.0 200.2 %shard_map.64 = bf16[2,64,64,256]{3,2,1,0:T(8,128)(2,1)} custom-call(bf16[2,64,64,256]{3,2,1,0:T(8,128)(2,1)} %x.1, f32[4,64,64]{2,1,0:T(8,128)} %phases.1, f32[4,256]{1,0:T(4,128)} %freqs.1, bf16[4,2,2,64,64]{4,3,2,1,0:T(8,128)(2,1)} %selfs.1, bf16[4,2,2,64,64]{4,3,2,1,0:T(8,128)(2,1)} %crosses.1, bf16[4,2,64,64]{3,2,1,0:T(8,128)(2,1)} %planes.1), custom_call_target="tpu_custom_call" | custom-call | flops 12884901888 | bytes 8388608 | tf_op jit(solution)/shard_map/pallas_call | solution.py:376
  200.2 4.8 %copy.8 = bf16[2,64,64,256]{3,2,1,0:T(8,128)(2,1)} copy(bf16[2,64,64,256]{3,2,1,0:T(8,128)(2,1)} %shard_map.64) | data formatting | bytes 8388608

commit v2 on v1

--- a/solution.py
+++ b/solution.py
@@ -13,7 +13,6 @@
 R = 64
 N = 8
 Q = R // N
-W = 3
 SINE = (
     6.283182621002197,
     -41.34142303466797,
@@ -25,9 +24,9 @@
 
 
 def kernel(
-    x, phases, freqs, selfs, crosses, planes, out,
-    stage, a, s, y, f, g, b2s, b2r, b3s, b3r, zb, tab, ostage, zphase, mats, mixes,
-    in_sem, ph_s, ph_r, zf_s, zf_r, y_s, y_r, c_s, c_r, x_s, x_r, zb_s, zb_r, out_sem,
+    x, phases_in, freqs, selfs_in, crosses_in, planes_in, out,
+    phases, selfs, crosses, planes, ownphase, stage, a, s, y, f, g, b2s, b2r, b3s, b3r, zb, tab, zphase, mats, mixes,
+    in_sem, ph_s, ph_r, zf_s, zf_r, y_s, y_r, c_s, c_r, x_s, x_r, zb_s, zb_r, mat_sem, gate,
 ):
     gr, gc = lax.axis_index("row"), lax.axis_index("col")
     nr, nc = lax.axis_size("row"), lax.axis_size("col")
@@ -36,6 +35,9 @@
     to_z = (gr, gc + nc // 2 - nc * half[1])
     to_c = (gr + 1 - 2 * half[2], gc)
     to_x = (gr, gc + 1 - 2 * half[3])
+    other = (gr, (gc + nc // 4) % nc)
+    late = (gc // (nc // 4)) % 2
+    other_back = (gr, (gc + nc - nc // 4) % nc)
 
     def lanes_of(which):
         return pl.ds(pl.multiple_of(which * 2 * R, 2 * R), 2 * R)
@@ -53,7 +55,12 @@
             device_id=to, device_id_type=MESH)
 
     def phase_copy():
-        return remote(phases, zphase, ph_s, ph_r, to_z)
+        return remote(ownphase, zphase, ph_s, ph_r, to_z)
+
+    def small_copy(n):
+        src = (phases_in, selfs_in, crosses_in, planes_in)[n]
+        dst = (phases, selfs, crosses, planes)[n]
+        return pltpu.make_async_copy(src, dst, mat_sem.at[n])
 
     def z_fwd(i):
         return remote(s.at[i], a.at[1, i], zf_s.at[i], zf_r.at[i], to_z)
@@ -73,25 +80,21 @@
     def z_back(i):
         return remote(s.at[i], zb.at[i], zb_s.at[i], zb_r.at[i], to_z)
 
-    def out_copy(side, j, lanes):
-        return pltpu.make_async_copy(
-            ostage.at[side * N + j],
-            out.at[:, pl.ds(pl.multiple_of(j * Q, Q), Q), :, lanes],
-            out_sem.at[side * N + j])
-
     def loop(n, body):
         lax.fori_loop(0, n, lambda i, c: (body(i), c)[1], 0)
 
-    for n in range(4):
+    load_copy(0, 0, theirs).start()
+    small_copy(0).start()
+    for n in range(1, 4):
         load_copy(n, 0, theirs).start()
     for n in range(4):
         load_copy(n, 1, mine).start()
+    for n in range(1, 4):
+        small_copy(n).start()
 
     barrier = pltpu.get_barrier_semaphore()
-    for to in (to_y, to_z, to_c, to_x):
+    for to in (to_y, to_z, to_c, to_x, other, other_back):
         pl.semaphore_signal(barrier, inc=1, device_id=to, device_id_type=MESH)
-    pl.semaphore_wait(barrier, 4)
-    phase_copy().start()
 
     lane = lax.broadcasted_iota(jnp.int32, (R, 2 * R), 1)
     low = lane < R
@@ -128,13 +131,36 @@
         y_copy(0, 2 * n + 1).start()
 
     pack_theirs(0)
-    z_fwd(0).start()
-    z_fwd(1).start()
-    pack_theirs(1)
-    z_fwd(2).start()
-    loop(2, lambda n: pack_theirs(n + 2))
+    pl.semaphore_wait(barrier, 6)
+
+    @pl.when(late == 0)
+    def _():
+        z_fwd(0).start()
+        z_fwd(1).start()
+
+    small_copy(0).wait()
+    for k in range(2):
+        ownphase[k] = jnp.concatenate([phases[2 * k], phases[2 * k + 1]], axis=1)
+    phase_copy().start()
+
+    def pack_next(n):
+        pack_theirs(n + 1)
+
+        @pl.when(late == 0)
+        def _():
+            z_fwd(2 * n + 2).start()
+            z_fwd(2 * n + 3).start()
+
+    loop(3, pack_next)
+
+    @pl.when(late == 0)
+    def _():
+        loop(N, lambda j: z_fwd(N + j).start())
+
     loop(4, pack_mine)
 
+    for n in range(1, 4):
+        small_copy(n).wait()
     for k in range(4):
         h = half[k]
         own = selfs[k, h]
@@ -158,12 +184,12 @@
             jnp.concatenate([im, re, re, -im], axis=1)], axis=0)
         mixes[k] = wide.T.astype(BF16)
 
-    sub = lax.broadcasted_iota(jnp.int32, (R, R), 0)
-    col = lax.broadcasted_iota(jnp.int32, (R, R), 1)
+    sub = lax.broadcasted_iota(jnp.int32, (R, 2 * R), 0)
     quarter = jnp.where(low, 0.0, 0.25)
 
     def table(k, grp, j):
-        ph = phases if grp == 0 else zphase
+        ph = ownphase if grp == 0 else zphase
+        first = k % 2 * R
         fr = freqs[pl.ds(k, 1), mine] * (0.5 / jnp.pi)
         low1 = lax.broadcasted_iota(jnp.int32, (1, 2 * R), 1) < R
         frs = (jnp.where(low1, fr, turn(fr)), jnp.where(low1, turn(fr), fr))
@@ -171,9 +197,9 @@
         def one(q):
             o = j * Q + q
             if k % 2 == 0:
-                picked = jnp.where(col == o, ph[k], 0.0)
+                picked = jnp.where(lane == o + first, ph[k // 2], 0.0)
             else:
-                picked = jnp.where(col == sub, ph[k, pl.ds(o, 1)], 0.0)
+                picked = jnp.where(lane == sub + first, ph[k // 2, pl.ds(o, 1)], 0.0)
             angle = jnp.sum(picked, axis=1, keepdims=True)
             for u in range(2):
                 t = angle * frs[u] + quarter
@@ -184,8 +210,11 @@
                     p = p * t2 + c
                 tab[k, grp, u * N + j, q] = (p * t).astype(BF16)
 
-        for q in range(Q):
-            one(q)
+        def some(n):
+            for d in range(4):
+                one(4 * n + d)
+
+        loop(Q // 4, some)
 
     def rotate(k, grp, i, q, p_, q_):
         t = tab[k, grp, i, q].astype(F32)
@@ -201,7 +230,8 @@
 
     def apart(k, grp, i, own, far, put):
         m = mats[k, pl.ds(0, 2 * R)]
-        for q in range(0, Q, 2):
+
+        def pair(q):
             v = [jnp.concatenate([own[q + d], far[q + d]], axis=0) for d in range(2)]
             pq = jnp.dot(m, jnp.concatenate(v, axis=1), preferred_element_type=F32)
             rows = [
@@ -212,6 +242,9 @@
             for d in range(2):
                 put(q + d, v[d * R:(d + 1) * R])
 
+        for q in range(0, Q, 2):
+            pair(q)
+
     def row_of(o):
         return pl.ds(pl.multiple_of(o * R, R), R)
 
@@ -227,7 +260,9 @@
 
     def level1(u, j):
         m = mats[1]
-        for q in range(0, Q, 2):
+
+        def pair(n):
+            q = 2 * n
             v = []
             for d in range(2):
                 o = j * Q + q + d
@@ -244,6 +279,9 @@
                 for d in range(2):
                     g[grp, row_of(j * Q + q + d)] = w[d * R:(d + 1) * R]
 
+        for n in range(Q // 2):
+            pair(n)
+
     def core_send(u, j):
         for grp in range(2):
             for q in range(Q):
@@ -277,66 +315,61 @@
     def merge(first, second, side, j, lanes):
         for q in range(Q):
             p0, p1 = first[q].astype(F32), second[q].astype(F32)
-            ostage[side * N + j, 0, q] = jnp.where(low, p0, turn(p1)).astype(BF16)
-            ostage[side * N + j, 1, q] = jnp.where(low, turn(p0), p1).astype(BF16)
-        out_copy(side, j, lanes).start()
-
-    def z_arrive(i, more):
+            out[0, j * Q + q, :, lanes] = jnp.where(low, p0, turn(p1)).astype(BF16)
+            out[1, j * Q + q, :, lanes] = jnp.where(low, turn(p0), p1).astype(BF16)
+
+    def z_arrive(i):
         z_fwd(i).wait()
-        if more:
-            z_fwd(i + W).start()
         y_copy(1, i).start()
 
-    phase_copy().wait()
-
-    def come0(j):
+    def early(j):
         for k in range(4):
             table(k, 0, j)
+        level0(0, 0, j)
+
+    loop(N, early)
+
+    @pl.when(late == 1)
+    def _():
+        pl.semaphore_wait(gate, 1)
+        loop(2 * N, lambda i: z_fwd(i).start())
+
+    phase_copy().wait()
+
+    def come(j):
+        z_arrive(j)
+
+        @pl.when((late == 0) & (j == 0))
+        def _():
+            pl.semaphore_signal(gate, inc=1, device_id=other, device_id_type=MESH)
+
+        for k in range(4):
             table(k, 1, j)
-        level0(0, 0, j)
-        z_arrive(j, True)
-
-    come0(0)
-
-    def come(j):
-        come0(j + 1)
-        level0(1, 0, j)
-
-    loop(N - 1, come)
+
+        @pl.when(j > 0)
+        def _():
+            level0(1, 0, j - 1)
+
+    loop(N, come)
     loop(N, lambda j: y_copy(0, N + j).start())
     level0(1, 0, N - 1)
 
-    loop(N // 2, lambda j: level1(0, j))
-    z_arrive(N, True)
-    loop(N // 2, lambda j: level1(0, j + N // 2))
-    z_arrive(N + 1, True)
+    loop(N, lambda j: level1(0, j))
+    loop(4, lambda j: z_arrive(N + j))
     loop(N, lambda j: core_send(0, j))
     loop(N, lambda j: level2(0, j))
-    z_arrive(N + 2, True)
+    loop(3, lambda j: z_arrive(N + 4 + j))
     loop(N, lambda j: x_send(0, j))
-    z_arrive(N + 3, True)
+    z_arrive(2 * N - 1)
     loop(N, lambda j: level0(0, 1, j))
 
-    def come1(j):
-        z_arrive(N + 4 + j, False)
-        level0(1, 1, j)
-        for d in range(2):
-            level3(1, 0, 2 * j + d)
-            x_copy(0, 0, 2 * j + d).start()
-
-    z_arrive(N + 4, True)
-    level0(1, 1, 0)
-    level3(1, 0, 0)
-    x_copy(0, 0, 0).start()
-    level3(1, 0, 1)
-    x_copy(0, 0, 1).start()
-    loop(1, lambda _: come1(1))
-    z_back(0).start()
-    loop(1, lambda _: come1(2))
-    z_back(1).start()
-    loop(1, lambda _: come1(3))
-    loop(N - 2, lambda j: z_back(j + 2).start())
-    loop(N - 4, lambda j: level0(1, 1, j + 4))
+    def back0(j):
+        level3(1, 0, j)
+        z_back(j).start()
+        x_copy(0, 0, j).start()
+
+    loop(N, back0)
+    loop(N, lambda j: level0(1, 1, j))
 
     loop(N, lambda j: level1(1, j))
     loop(N, lambda j: core_send(1, j))
@@ -363,8 +396,17 @@
         merge(zb.at[j], zb.at[N + j], 1, j, theirs)
 
     loop(N, last)
-    loop(N, lambda j: out_copy(0, j, mine).wait())
-    loop(N, lambda j: out_copy(1, j, theirs).wait())
+
+
+def flush(src, dst, sem):
+    copies = []
+    for n in range(2 * N):
+        part = (n // N, pl.ds(n % N * Q, Q))
+        copies.append(pltpu.make_async_copy(src.at[part], dst.at[part], sem.at[n]))
+    for copy in copies:
+        copy.start()
+    for copy in copies:
+        copy.wait()
 
 
 def local(field, phases, frequencies, self_mats, cross_mats, plane_mats):
@@ -373,12 +415,17 @@
     chunk = (Q, R, 2 * R)
     unit2 = (2 * N,) + chunk
     dma = pltpu.SemaphoreType.DMA
-    return pl.pallas_call(
+    result = pl.pallas_call(
         kernel,
-        out_shape=jax.ShapeDtypeStruct(field.shape, field.dtype),
-        in_specs=[anywhere, vm, vm, vm, vm, vm],
-        out_specs=anywhere,
+        out_shape=pltpu.VMEM(field.shape, field.dtype),
+        in_specs=[anywhere, anywhere, vm, anywhere, anywhere, anywhere],
+        out_specs=vm,
         scratch_shapes=[
+            pltpu.VMEM(phases.shape, F32),
+            pltpu.VMEM(self_mats.shape, BF16),
+            pltpu.VMEM(cross_mats.shape, BF16),
+            pltpu.VMEM(plane_mats.shape, BF16),
+            pltpu.VMEM((2, R, 2 * R), F32),
             pltpu.VMEM((8, 2, R, 16, 2 * R), BF16),
             pltpu.VMEM((2,) + unit2, BF16),
             pltpu.VMEM(unit2, BF16),
@@ -391,19 +438,27 @@
             pltpu.VMEM((2,) + unit2, BF16),
             pltpu.VMEM(unit2, BF16),
             pltpu.VMEM((4, 2) + unit2, BF16),
-            pltpu.VMEM((2 * N, 2) + chunk, BF16),
-            pltpu.VMEM((4, R, R), F32),
+            pltpu.VMEM((2, R, 2 * R), F32),
             pltpu.VMEM((4, 4 * R, 2 * R), BF16),
             pltpu.VMEM((4, 4 * R, 2 * R), BF16),
             dma((8,)), dma, dma, dma((2 * N,)), dma((2 * N,)),
             dma((4 * N,)), dma((4 * N,)), dma((4 * N,)), dma((4 * N,)),
-            dma((4 * N,)), dma((4 * N,)), dma((2 * N,)), dma((2 * N,)), dma((2 * N,)),
+            dma((4 * N,)), dma((4 * N,)), dma((2 * N,)), dma((2 * N,)),
+            dma((4,)), pltpu.SemaphoreType.REGULAR,
         ],
         compiler_params=pltpu.CompilerParams(
-            collective_id=0, has_side_effects=True, vmem_limit_bytes=62 * 2**20),
+            collective_id=0, has_side_effects=True, vmem_limit_bytes=58 * 2**20),
         cost_estimate=pl.CostEstimate(
             flops=12 * 2**30, bytes_accessed=2**23, transcendentals=2**23),
     )(field, phases, frequencies, self_mats, cross_mats, plane_mats)
+    return pl.pallas_call(
+        flush,
+        out_shape=jax.ShapeDtypeStruct(field.shape, field.dtype),
+        in_specs=[vm],
+        out_specs=anywhere,
+        scratch_shapes=[dma((2 * N,))],
+        cost_estimate=pl.CostEstimate(flops=0, bytes_accessed=2**22, transcendentals=0),
+    )(result)
 
 
 def solution(mesh):

time: 209 us -> 208 us (level); the launches traced: 205 us -> 208 us
  Pallas kernels: 200 us -> 206 us
  local copies, waits for them, and re-layouts: 4.79 us -> 1.93 us
    pallas_call x1 -> x2, Pallas kernels: 200 us -> 206 us  [the longest x1 202 us: local(): pl.pallas_call(kernel, out_shape=pltpu.VMEM(field.shape, field.dtype), in...]
    unnamed x1 -> x2, local copies, waits for them, and re-layouts: 4.79 us -> 1.93 us
where the time goes in v2:
time: 208 us
  Pallas kernels  206 us (99%)
    pallas_call x1, Pallas kernels, local(): pl.pallas_call(kernel, out_shape=pltpu.VMEM(field.shape, field.dtype), in...  202 us
    pallas_call x1, Pallas kernels, local(): pl.pallas_call(flush, out_shape=jax.ShapeDtypeStruct(field.shape, field.d...  4.32 us

profile of v2, /device:TPU:96, one launch (start us, length us, event | category | flops | bytes accessed | tf_op | source)
XLA Modules:
  0.0 207.9 jit_solution(11236857365819040199)
XLA Ops:
  0.0 201.6 %shard_map.64.src = bf16[2,64,64,256]{3,2,1,0:T(8,128)(2,1)S(1)} custom-call(bf16[2,64,64,256]{3,2,1,0:T(8,128)(2,1)} %x.1, f32[4,64,64]{2,1,0:T(8,128)} %phases_in.1, f32[4,256]{1,0:T(4,128)} %freqs.1, bf16[4,2,2,64,64]{4,3,2,1,0:T(8,128)(2,1)} %selfs_in.1, bf16[4,2,2,64,64]{4,3,2,1,0:T(8,128)(2,1)} %crosses_in.1, bf16[4,2,64,64]{3,2,1,0:T(8,128)(2,1)} %planes_in.1), custom_call_target="tpu_custom_call" | custom-call | flops 12884901888 | bytes 8388608 | tf_op jit(solution)/shard_map/pallas_call | solution.py:418
  201.7 0.0 copy-start
  201.7 1.9 copy-done
  203.6 4.3 %shard_map.65 = bf16[2,64,64,256]{3,2,1,0:T(8,128)(2,1)} custom-call(bf16[2,64,64,256]{3,2,1,0:T(8,128)(2,1)} %copy-done), custom_call_target="tpu_custom_call" | custom-call | bytes 4194304 | tf_op jit(solution)/shard_map/pallas_call | solution.py:454
Async XLA Ops:
  201.7 1.9 copy-start

commit v3 on v2

--- a/solution.py
+++ b/solution.py
@@ -24,8 +24,8 @@
 
 
 def kernel(
-    x, phases_in, freqs, selfs_in, crosses_in, planes_in, out,
-    phases, selfs, crosses, planes, ownphase, stage, a, s, y, f, g, b2s, b2r, b3s, b3r, zb, tab, zphase, mats, mixes,
+    x, phases_in, freqs_in, selfs_in, crosses_in, planes_in, out,
+    phases, freqs, selfs, crosses, planes, ownphase, a, s, y, f, g, b2r, b3r, zb, tab, zphase, mats, mixes,
     in_sem, ph_s, ph_r, zf_s, zf_r, y_s, y_r, c_s, c_r, x_s, x_r, zb_s, zb_r, mat_sem, gate,
 ):
     gr, gc = lax.axis_index("row"), lax.axis_index("col")
@@ -47,7 +47,7 @@
     def load_copy(n, side, lanes):
         return pltpu.make_async_copy(
             x.at[:, :, pl.ds(pl.multiple_of(n * 16, 16), 16), lanes],
-            stage.at[side * 4 + n], in_sem.at[side * 4 + n])
+            tab.at[side * 4 + n], in_sem.at[side * 4 + n])
 
     def remote(src, dst, ssem, rsem, to):
         return pltpu.make_async_remote_copy(
@@ -58,24 +58,27 @@
         return remote(ownphase, zphase, ph_s, ph_r, to_z)
 
     def small_copy(n):
-        src = (phases_in, selfs_in, crosses_in, planes_in)[n]
-        dst = (phases, selfs, crosses, planes)[n]
+        src = (phases_in, freqs_in, selfs_in, crosses_in, planes_in)[n]
+        dst = (phases, freqs, selfs, crosses, planes)[n]
         return pltpu.make_async_copy(src, dst, mat_sem.at[n])
 
     def z_fwd(i):
         return remote(s.at[i], a.at[1, i], zf_s.at[i], zf_r.at[i], to_z)
 
     def y_copy(grp, i):
-        n = grp * 2 * N + i
-        return remote(a.at[grp, i], y.at[grp, i], y_s.at[n], y_r.at[n], to_y)
-
-    def c_copy(grp, u, j):
-        n = grp * 2 * N + u * N + j
-        return remote(b2s.at[grp, j], b2r.at[grp, u * N + j], c_s.at[n], c_r.at[n], to_c)
+        return remote(a.at[grp, i], y.at[grp, i], y_s.at[i], y_r.at[i], to_y)
+
+    def y_own(n):
+        part = (0, pl.ds(2 * n, 2))
+        return remote(a.at[part], y.at[part], y_s.at[2 * N + n], y_r.at[2 * N + n], to_y)
+
+    def c_copy(u, j):
+        n = u * N + j
+        return remote(y.at[:, n], b2r.at[:, n], c_s.at[n], c_r.at[n], to_c)
 
     def x_copy(grp, u, j):
         n = grp * 2 * N + u * N + j
-        return remote(b3s.at[grp, j], b3r.at[grp, u * N + j], x_s.at[n], x_r.at[n], to_x)
+        return remote(a.at[grp, u * N + j], b3r.at[grp, u * N + j], x_s.at[n], x_r.at[n], to_x)
 
     def z_back(i):
         return remote(s.at[i], zb.at[i], zb_s.at[i], zb_r.at[i], to_z)
@@ -83,13 +86,12 @@
     def loop(n, body):
         lax.fori_loop(0, n, lambda i, c: (body(i), c)[1], 0)
 
-    load_copy(0, 0, theirs).start()
     small_copy(0).start()
-    for n in range(1, 4):
+    for n in range(4):
         load_copy(n, 0, theirs).start()
     for n in range(4):
         load_copy(n, 1, mine).start()
-    for n in range(1, 4):
+    for n in range(1, 5):
         small_copy(n).start()
 
     barrier = pltpu.get_barrier_semaphore()
@@ -103,8 +105,8 @@
         return pltpu.roll(v, R, 1)
 
     def pack(n, side, put):
-        f[0, pl.ds(0, R * 16)] = stage[side * 4 + n, 0].reshape(R * 16, 2 * R).astype(F32)
-        f[1, pl.ds(0, R * 16)] = stage[side * 4 + n, 1].reshape(R * 16, 2 * R).astype(F32)
+        f[0, pl.ds(0, R * 16)] = tab[side * 4 + n, 0].reshape(R * 16, 2 * R).astype(F32)
+        f[1, pl.ds(0, R * 16)] = tab[side * 4 + n, 1].reshape(R * 16, 2 * R).astype(F32)
         for k in range(16):
             re = f[0, pl.ds(k, R, stride=16)]
             im = f[1, pl.ds(k, R, stride=16)]
@@ -127,22 +129,20 @@
     def pack_mine(n):
         load_copy(n, 1, mine).wait()
         pack(n, 1, put_a)
-        y_copy(0, 2 * n).start()
-        y_copy(0, 2 * n + 1).start()
-
+        y_own(n).start()
+
+    small_copy(0).wait()
+    for k in range(2):
+        ownphase[k] = jnp.concatenate([phases[2 * k], phases[2 * k + 1]], axis=1)
+    pl.semaphore_wait(barrier, 6)
+    phase_copy().start()
     pack_theirs(0)
-    pl.semaphore_wait(barrier, 6)
 
     @pl.when(late == 0)
     def _():
         z_fwd(0).start()
         z_fwd(1).start()
 
-    small_copy(0).wait()
-    for k in range(2):
-        ownphase[k] = jnp.concatenate([phases[2 * k], phases[2 * k + 1]], axis=1)
-    phase_copy().start()
-
     def pack_next(n):
         pack_theirs(n + 1)
 
@@ -159,7 +159,7 @@
 
     loop(4, pack_mine)
 
-    for n in range(1, 4):
+    for n in range(1, 5):
         small_copy(n).wait()
     for k in range(4):
         h = half[k]
@@ -187,12 +187,15 @@
     sub = lax.broadcasted_iota(jnp.int32, (R, 2 * R), 0)
     quarter = jnp.where(low, 0.0, 0.25)
 
-    def table(k, grp, j):
+    def tab_at(k, grp, j, q):
+        return ((k * 2 + grp) * 2 + j // 4, j // 2 % 2, pl.ds(j % 2 * 32 + q * 4, 4))
+
+    def table(k, grp, u, j):
         ph = ownphase if grp == 0 else zphase
         first = k % 2 * R
         fr = freqs[pl.ds(k, 1), mine] * (0.5 / jnp.pi)
         low1 = lax.broadcasted_iota(jnp.int32, (1, 2 * R), 1) < R
-        frs = (jnp.where(low1, fr, turn(fr)), jnp.where(low1, turn(fr), fr))
+        frs = jnp.where(low1, fr, turn(fr)) if u == 0 else jnp.where(low1, turn(fr), fr)
 
         def one(q):
             o = j * Q + q
@@ -201,23 +204,19 @@
             else:
                 picked = jnp.where(lane == sub + first, ph[k // 2, pl.ds(o, 1)], 0.0)
             angle = jnp.sum(picked, axis=1, keepdims=True)
-            for u in range(2):
-                t = angle * frs[u] + quarter
-                t = t - jnp.round(t)
-                t2 = t * t
-                p = SINE[5]
-                for c in SINE[4::-1]:
-                    p = p * t2 + c
-                tab[k, grp, u * N + j, q] = (p * t).astype(BF16)
-
-        def some(n):
-            for d in range(4):
-                one(4 * n + d)
-
-        loop(Q // 4, some)
-
-    def rotate(k, grp, i, q, p_, q_):
-        t = tab[k, grp, i, q].astype(F32)
+            t = angle * frs + quarter
+            t = t - jnp.round(t)
+            t2 = t * t
+            p = SINE[5]
+            for c in SINE[4::-1]:
+                p = p * t2 + c
+            tab[tab_at(k, grp, j, q)] = (p * t).astype(BF16).reshape(4, 16, 2 * R)
+
+        for q in range(Q):
+            one(q)
+
+    def rotate(k, grp, j, q, p_, q_):
+        t = tab[tab_at(k, grp, j, q)].reshape(R, 2 * R).astype(F32)
         r = turn(t)
         sine = jnp.where(low, t, r)
         cosine = jnp.where(low, r, t)
@@ -228,14 +227,14 @@
     def mix(k, rows):
         return jnp.dot(jnp.concatenate(rows, axis=0), mixes[k], preferred_element_type=F32)
 
-    def apart(k, grp, i, own, far, put):
+    def apart(k, grp, j, own, far, put):
         m = mats[k, pl.ds(0, 2 * R)]
 
         def pair(q):
             v = [jnp.concatenate([own[q + d], far[q + d]], axis=0) for d in range(2)]
             pq = jnp.dot(m, jnp.concatenate(v, axis=1), preferred_element_type=F32)
             rows = [
-                rotate(k, grp, i, q + d, pq[:R, d * 2 * R:(d + 1) * 2 * R],
+                rotate(k, grp, j, q + d, pq[:R, d * 2 * R:(d + 1) * 2 * R],
                        pq[R:, d * 2 * R:(d + 1) * 2 * R])
                 for d in range(2)]
             v = mix(k, rows)
@@ -255,8 +254,13 @@
 
     def level0(grp, u, j):
         i = u * N + j
-        y_copy(grp, i).wait()
-        apart(0, grp, i, a.at[grp, i], y.at[grp, i], put_f(grp, j))
+        if grp == 0:
+            @pl.when(j % 2 == 0)
+            def _():
+                y_own(i // 2).wait()
+        else:
+            y_copy(grp, i).wait()
+        apart(0, grp, j, a.at[grp, i], y.at[grp, i], put_f(grp, j))
 
     def level1(u, j):
         m = mats[1]
@@ -271,7 +275,7 @@
             pq = jnp.dot(m, jnp.concatenate(v, axis=1), preferred_element_type=F32)
             for grp in range(2):
                 rows = [
-                    rotate(1, grp, u * N + j, q + d,
+                    rotate(1, grp, j, q + d,
                            pq[grp * 2 * R:grp * 2 * R + R, d * 2 * R:(d + 1) * 2 * R],
                            pq[grp * 2 * R + R:(grp + 1) * 2 * R, d * 2 * R:(d + 1) * 2 * R])
                     for d in range(2)]
@@ -285,22 +289,22 @@
     def core_send(u, j):
         for grp in range(2):
             for q in range(Q):
-                b2s[grp, j, q] = g[grp, pl.ds(j * Q + q, R, stride=R)].astype(BF16)
-            c_copy(grp, u, j).start()
+                y[grp, u * N + j, q] = g[grp, pl.ds(j * Q + q, R, stride=R)].astype(BF16)
+        c_copy(u, j).start()
 
     def level2(u, j):
+        c_copy(u, j).wait()
         for grp in range(2):
-            c_copy(grp, u, j).wait()
-            apart(2, grp, u * N + j, b2s.at[grp, j], b2r.at[grp, u * N + j], put_f(grp, j))
-
-    def x_pack(grp, j):
+            apart(2, grp, j, y.at[grp, u * N + j], b2r.at[grp, u * N + j], put_f(grp, j))
+
+    def x_pack(grp, u, j):
         for q in range(Q):
-            b3s[grp, j, q] = f[grp, pl.ds(j * Q + q, R, stride=R)].astype(BF16)
+            a[grp, u * N + j, q] = f[grp, pl.ds(j * Q + q, R, stride=R)].astype(BF16)
 
     def x_send(u, j):
-        x_pack(1, j)
+        x_pack(1, u, j)
         x_copy(1, u, j).start()
-        x_pack(0, j)
+        x_pack(0, u, j)
 
     def level3(grp, u, j):
         i = u * N + j
@@ -310,7 +314,7 @@
             dst[q] = v.astype(BF16)
 
         x_copy(grp, u, j).wait()
-        apart(3, grp, i, b3s.at[grp, j], b3r.at[grp, i], put)
+        apart(3, grp, j, a.at[grp, i], b3r.at[grp, i], put)
 
     def merge(first, second, side, j, lanes):
         for q in range(Q):
@@ -324,7 +328,7 @@
 
     def early(j):
         for k in range(4):
-            table(k, 0, j)
+            table(k, 0, 0, j)
         level0(0, 0, j)
 
     loop(N, early)
@@ -344,14 +348,14 @@
             pl.semaphore_signal(gate, inc=1, device_id=other, device_id_type=MESH)
 
         for k in range(4):
-            table(k, 1, j)
+            table(k, 1, 0, j)
 
         @pl.when(j > 0)
         def _():
             level0(1, 0, j - 1)
 
     loop(N, come)
-    loop(N, lambda j: y_copy(0, N + j).start())
+    loop(N // 2, lambda n: y_own(N // 2 + n).start())
     level0(1, 0, N - 1)
 
     loop(N, lambda j: level1(0, j))
@@ -361,21 +365,29 @@
     loop(3, lambda j: z_arrive(N + 4 + j))
     loop(N, lambda j: x_send(0, j))
     z_arrive(2 * N - 1)
-    loop(N, lambda j: level0(0, 1, j))
 
     def back0(j):
         level3(1, 0, j)
         z_back(j).start()
         x_copy(0, 0, j).start()
+        for k in range(3):
+            table(k, 0, 1, j)
+            table(k, 1, 1, j)
+        level0(0, 1, j)
 
     loop(N, back0)
     loop(N, lambda j: level0(1, 1, j))
-
     loop(N, lambda j: level1(1, j))
     loop(N, lambda j: core_send(1, j))
     loop(N, lambda j: level2(1, j))
-    loop(N, lambda j: level3(0, 0, j))
     loop(N, lambda j: x_send(1, j))
+
+    def end0(j):
+        level3(0, 0, j)
+        table(3, 0, 1, j)
+        table(3, 1, 1, j)
+
+    loop(N, end0)
 
     def back1(j):
         level3(1, 1, j)
@@ -396,17 +408,6 @@
         merge(zb.at[j], zb.at[N + j], 1, j, theirs)
 
     loop(N, last)
-
-
-def flush(src, dst, sem):
-    copies = []
-    for n in range(2 * N):
-        part = (n // N, pl.ds(n % N * Q, Q))
-        copies.append(pltpu.make_async_copy(src.at[part], dst.at[part], sem.at[n]))
-    for copy in copies:
-        copy.start()
-    for copy in copies:
-        copy.wait()
 
 
 def local(field, phases, frequencies, self_mats, cross_mats, plane_mats):
@@ -415,50 +416,40 @@
     chunk = (Q, R, 2 * R)
     unit2 = (2 * N,) + chunk
     dma = pltpu.SemaphoreType.DMA
-    result = pl.pallas_call(
+    return pl.pallas_call(
         kernel,
         out_shape=pltpu.VMEM(field.shape, field.dtype),
-        in_specs=[anywhere, anywhere, vm, anywhere, anywhere, anywhere],
+        in_specs=[anywhere] * 6,
         out_specs=vm,
         scratch_shapes=[
             pltpu.VMEM(phases.shape, F32),
+            pltpu.VMEM(frequencies.shape, F32),
             pltpu.VMEM(self_mats.shape, BF16),
             pltpu.VMEM(cross_mats.shape, BF16),
             pltpu.VMEM(plane_mats.shape, BF16),
             pltpu.VMEM((2, R, 2 * R), F32),
-            pltpu.VMEM((8, 2, R, 16, 2 * R), BF16),
             pltpu.VMEM((2,) + unit2, BF16),
             pltpu.VMEM(unit2, BF16),
             pltpu.VMEM((2,) + unit2, BF16),
             pltpu.VMEM((2, R * R, 2 * R), F32),
             pltpu.VMEM((2, R * R, 2 * R), F32),
-            pltpu.VMEM((2, N) + chunk, BF16),
             pltpu.VMEM((2,) + unit2, BF16),
-            pltpu.VMEM((2, N) + chunk, BF16),
             pltpu.VMEM((2,) + unit2, BF16),
             pltpu.VMEM(unit2, BF16),
-            pltpu.VMEM((4, 2) + unit2, BF16),
+            pltpu.VMEM((16, 2, R, 16, 2 * R), BF16),
             pltpu.VMEM((2, R, 2 * R), F32),
             pltpu.VMEM((4, 4 * R, 2 * R), BF16),
             pltpu.VMEM((4, 4 * R, 2 * R), BF16),
             dma((8,)), dma, dma, dma((2 * N,)), dma((2 * N,)),
-            dma((4 * N,)), dma((4 * N,)), dma((4 * N,)), dma((4 * N,)),
+            dma((3 * N,)), dma((3 * N,)), dma((2 * N,)), dma((2 * N,)),
             dma((4 * N,)), dma((4 * N,)), dma((2 * N,)), dma((2 * N,)),
-            dma((4,)), pltpu.SemaphoreType.REGULAR,
+            dma((5,)), pltpu.SemaphoreType.REGULAR,
         ],
         compiler_params=pltpu.CompilerParams(
-            collective_id=0, has_side_effects=True, vmem_limit_bytes=58 * 2**20),
+            collective_id=0, has_side_effects=True, vmem_limit_bytes=43 * 2**20),
         cost_estimate=pl.CostEstimate(
             flops=12 * 2**30, bytes_accessed=2**23, transcendentals=2**23),
     )(field, phases, frequencies, self_mats, cross_mats, plane_mats)
-    return pl.pallas_call(
-        flush,
-        out_shape=jax.ShapeDtypeStruct(field.shape, field.dtype),
-        in_specs=[vm],
-        out_specs=anywhere,
-        scratch_shapes=[dma((2 * N,))],
-        cost_estimate=pl.CostEstimate(flops=0, bytes_accessed=2**22, transcendentals=0),
-    )(result)
 
 
 def solution(mesh):

time: 208 us -> 210 us (level)
  local copies, waits for them, and re-layouts: 1.93 us -> 8.6 us
  Pallas kernels: 206 us -> 200 us
    unnamed x2 -> x13, local copies, waits for them, and re-layouts: 1.93 us -> 8.6 us
    pallas_call x1 -> x0, Pallas kernels: 4.32 us -> none  [local(): pl.pallas_call(flush, out_shape=jax.ShapeDtypeStruct(field.shape, field.d...]
where the time goes in v3:
time: 210 us; the launch traced here: 209 us
  Pallas kernels  200 us (95%)
  local copies, waits for them, and re-layouts  8.6 us (4%)
    pallas_call x1, Pallas kernels, local(): pl.pallas_call(kernel, out_shape=pltpu.VMEM(field.shape, field.dtype), in...  200 us
    unnamed x13, local copies, waits for them, and re-layouts  8.6 us

profile of v3, /device:TPU:96, one launch (start us, length us, event | category | flops | bytes accessed | tf_op | source)
XLA Modules:
  0.0 208.6 jit_solution(6038573821723717729)
XLA Ops:
  0.0 0.0 copy-start
  0.0 2.2 %copy-done = bf16[2,64,64,256]{3,2,1,0:T(8,128)(2,1)S(1)} copy-done((bf16[2,64,64,256]{3,2,1,0:T(8,128)(2,1)S(1)}, bf16[2,64,64,256]{3,2,1,0:T(8,128)(2,1)}, u32[]{:S(2)}) %copy-start) | copy-done | bytes 4194328
  2.2 0.0 copy-start.1
  2.2 0.9 copy-done.1
  3.1 0.0 copy-start.2
  3.1 0.9 copy-done.2
  4.1 0.0 copy-start.3
  4.1 0.9 copy-done.3
  5.0 0.0 copy-start.4
  5.0 0.9 copy-done.4
  5.9 0.0 copy-start.5
  5.9 0.7 copy-done.5
  6.6 200.0 %shard_map.64 = bf16[2,64,64,256]{3,2,1,0:T(8,128)(2,1)S(1)} custom-call(bf16[2,64,64,256]{3,2,1,0:T(8,128)(2,1)S(1)} %copy-done, f32[4,64,64]{2,1,0:T(8,128)S(1)} %copy-done.3, f32[4,256]{1,0:T(4,128)S(1)} %copy-done.5, bf16[4,2,2,64,64]{4,3,2,1,0:T(8,128)(2,1)S(1)} %copy-done.1, bf16[4,2,2,64,64]{4,3,2,1,0:T(8,128)(2,1)S(1)} %copy-done.2, ...), custom_call_target="tpu_custom_call" | custom-call | flops 12884901888 | bytes 8388608 | tf_op jit(solution)/shard_map/pallas_call | solution.py:419
  206.6 2.0 copy.8
Async XLA Ops:
  0.0 2.2 %copy-start = (bf16[2,64,64,256]{3,2,1,0:T(8,128)(2,1)S(1)}, bf16[2,64,64,256]{3,2,1,0:T(8,128)(2,1)}, u32[]{:S(2)}) copy-start(bf16[2,64,64,256]{3,2,1,0:T(8,128)(2,1)} %x.1) | copy-start | bytes 12582916
  2.2 0.9 copy-start.1
  3.1 0.9 copy-start.2
  4.1 0.9 copy-start.3
  5.0 0.9 copy-start.4
  5.9 0.7 copy-start.5

commit v4 on v3

--- a/solution.py
+++ b/solution.py
@@ -446,7 +446,7 @@
             dma((5,)), pltpu.SemaphoreType.REGULAR,
         ],
         compiler_params=pltpu.CompilerParams(
-            collective_id=0, has_side_effects=True, vmem_limit_bytes=43 * 2**20),
+            collective_id=0, has_side_effects=True, vmem_limit_bytes=58 * 2**20),
         cost_estimate=pl.CostEstimate(
             flops=12 * 2**30, bytes_accessed=2**23, transcendentals=2**23),
     )(field, phases, frequencies, self_mats, cross_mats, plane_mats)

time: 210 us -> 202 us (0.962)
  local copies, waits for them, and re-layouts: 8.6 us -> 2.02 us
    unnamed x13 -> x1, local copies, waits for them, and re-layouts: 8.6 us -> 2.02 us
where the time goes in v4:
time: 202 us; the launch traced here: 201 us
  Pallas kernels  199 us (99%)
  local copies, waits for them, and re-layouts  2.02 us (1%)
    pallas_call x1, Pallas kernels, local(): pl.pallas_call(kernel, out_shape=pltpu.VMEM(field.shape, field.dtype), in...  199 us

profile of v4, /device:TPU:96, one launch (start us, length us, event | category | flops | bytes accessed | tf_op | source)
XLA Modules:
  0.0 200.9 jit_solution(3041365697110763222)
XLA Ops:
  0.0 198.9 %shard_map.64 = bf16[2,64,64,256]{3,2,1,0:T(8,128)(2,1)S(1)} custom-call(bf16[2,64,64,256]{3,2,1,0:T(8,128)(2,1)} %x.1, f32[4,64,64]{2,1,0:T(8,128)} %phases_in.1, f32[4,256]{1,0:T(4,128)} %freqs_in.1, bf16[4,2,2,64,64]{4,3,2,1,0:T(8,128)(2,1)} %selfs_in.1, bf16[4,2,2,64,64]{4,3,2,1,0:T(8,128)(2,1)} %crosses_in.1, bf16[4,2,64,64]{3,2,1,0:T(8,128)(2,1)} %planes_in.1), custom_call_target="tpu_custom_call" | custom-call | flops 12884901888 | bytes 8388608 | tf_op jit(solution)/shard_map/pallas_call | solution.py:419
  198.9 2.0 %copy.8 = bf16[2,64,64,256]{3,2,1,0:T(8,128)(2,1)} copy(bf16[2,64,64,256]{3,2,1,0:T(8,128)(2,1)S(1)} %shard_map.64) | data formatting | bytes 8388608
